TPU v7x, 32 devices: a whole 2x2x4 slice. The times are simulated.
32 devices in a mesh: groups: 2 (over y), tok: 4 (over x, core), hid: 4 (over z).
Axes of the slice: x: 2, y: 2, z: 4, core: 2. Of those that a mesh axis runs over, the one named last changes fastest.
Arguments:
- states: bfloat16 [8192, 5376], P(('groups', 'tok'), 'hid'), parts along dimension 0, may hold values from -6 to 6
- w_qkv: bfloat16 [5376, 8, 512], P('tok', 'hid'), may hold values from -0.078125 to 0.078125
- w_out: bfloat16 [2048, 5376], P('tok', 'hid'), may hold values from -0.125 to 0.125
- q_gain: float32 [128], replicated, may hold values from 0.5 to 14, as said below
- k_gain: float32 [128], replicated, may hold values from 0.5 to 14, as said below
Outputs:
- attended: bfloat16 [8192, 5376], P(('groups', 'tok'), 'hid'), parts along dimension 0
There are 2 independent parts, one for each index of `groups`. A program takes and returns all parts, laid end to end along the dimension named above; an argument that names none is the same for every part. Nothing has to cross between parts.
Inputs may be any that keep to these rules, and one draw needn't show every extreme that they name: `q_gain`: entries are positive. `k_gain`: entries are positive.
All inputs are finite; a program needn't handle non-finite values.
Results may differ from a plain program's by a relative error of at most 0.017.
The roundings to bfloat16 on the way count: a program that leaves them out, or rounds other values in their place, can miss the bound.
Values may be sent and summed in bfloat16 or wider, within the bound.
A program may use at most 128 MiB of HBM per device.

v0:
```python
import math
import jax
import jax.numpy as jnp
from jax import lax
from jax.sharding import PartitionSpec as P

HD = 128
GROUP = 2
WINDOW = 1024
EPS = 1e-06
SCALE = 168.0 ** (-0.5)
ROPE_BASE = 10000.0


def from_behind(value, axis, steps):
    count = lax.axis_size(axis)
    first, last = (max(0, -steps), min(count, count - steps))
    return lax.ppermute(value, axis, [(source, source + steps) for source in range(first, last)])


def head_norm(values, gain):
    meansq = jnp.mean(values * values, axis=-1, keepdims=True)
    return values * lax.rsqrt(meansq + EPS) * gain


def rotate(values, pos):
    half = values.shape[-1] // 2
    inverse = jnp.exp(
        jnp.arange(half, dtype=jnp.float32) * (-2.0 * math.log(ROPE_BASE) / values.shape[-1])
    )
    angle = pos.astype(jnp.float32)[:, None] * inverse[None, :]
    shape = (angle.shape[0],) + (1,) * (values.ndim - 2) + (half,)
    cosine = jnp.cos(angle).reshape(shape)
    sine = jnp.sin(angle).reshape(shape)
    first = values[..., :half]
    second = values[..., half:]
    return jnp.concatenate(
        [first * cosine - second * sine, second * cosine + first * sine], axis=-1
    )


def attend(query, keys, values, q_first, k_first):
    scores = jnp.einsum("qhgd,khd->hgqk", query, keys, preferred_element_type=jnp.float32) * SCALE
    q_index = q_first + jnp.arange(query.shape[0], dtype=jnp.int32)
    k_index = k_first + jnp.arange(keys.shape[0], dtype=jnp.int32)
    keep = (
        (k_index[None, :] <= q_index[:, None])
        & (q_index[:, None] - k_index[None, :] < WINDOW)
        & (k_index[None, :] >= 0)
    )
    masked = jnp.where(keep, scores, jnp.float32(-1e30))
    top = jnp.max(masked, axis=-1, keepdims=True)
    expo = jnp.where(keep, jnp.exp(masked - top), jnp.float32(0.0))
    total = jnp.sum(expo, axis=-1, keepdims=True)
    weights = (expo / total).astype(jnp.bfloat16)
    result = jnp.einsum("hgqk,khd->qhgd", weights, values, preferred_element_type=jnp.float32)
    return result.astype(jnp.bfloat16)


def on_device(states, w_qkv, w_out, q_gain, k_gain):
    rows = states.shape[0]
    kv_local = w_qkv.shape[1]
    columns = kv_local * (GROUP + 2) * HD
    weight_whole = lax.all_gather(w_qkv, "tok", axis=0, tiled=True).reshape(-1, columns)
    weight_part = weight_whole
    qkv = jnp.dot(
        lax.all_gather(states, "hid", axis=1, tiled=True),
        weight_part,
        preferred_element_type=jnp.float32,
    )
    qkv = qkv.reshape(rows, kv_local, GROUP + 2, HD)
    base = lax.axis_index("tok") * rows
    pos = base + jnp.arange(rows, dtype=jnp.int32)
    query = rotate(head_norm(qkv[:, :, :GROUP], q_gain), pos).astype(jnp.bfloat16)
    keys = rotate(head_norm(qkv[:, :, GROUP], k_gain), pos).astype(jnp.bfloat16)
    values = qkv[:, :, GROUP + 1].astype(jnp.bfloat16)
    paired = jnp.stack([keys, values], axis=1).reshape(rows, 2 * kv_local * HD)
    hops = max(1, WINDOW // rows)
    reach = min(WINDOW, rows)
    pieces = []
    current = paired
    current = from_behind(current, "tok", 1)
    pieces.insert(0, current)
    combined = jnp.concatenate(pieces + [paired], axis=0).reshape(-1, 2, kv_local, HD)
    reach_back = hops * reach
    block = 512
    outputs = []
    for index in range(rows // block):
        q_block = query[index * block : (index + 1) * block]
        kv_block = combined[index * block : index * block + block + reach_back]
        outputs.append(
            attend(
                q_block,
                kv_block[:, 0],
                kv_block[:, 1],
                base + index * block,
                base + index * block - reach_back,
            )
        )
    heads_out = jnp.concatenate(outputs, axis=0)
    heads_out = heads_out.reshape(rows, kv_local * GROUP * HD)
    out_whole = lax.all_gather(w_out, "tok", axis=0, tiled=True)
    weight_part = out_whole
    summed = jnp.dot(
        lax.all_gather(heads_out, "hid", axis=1, tiled=True),
        weight_part,
        preferred_element_type=jnp.float32,
    )
    return summed.astype(jnp.bfloat16)


def solution(mesh):
    return jax.shard_map(
        on_device,
        mesh=mesh,
        in_specs=(P(("groups", "tok"), "hid"), P("tok", "hid", None), P("tok", "hid"), P(), P()),
        out_specs=P(("groups", "tok"), "hid"),
        check_vma=False,
    )
```

profile of v0, /device:TPU:0, one launch (start us, length us, event | category | flops | bytes accessed | tf_op | source)
XLA Modules:
  0.0 458.9 jit_solution(5258725831197770475)
XLA Ops:
  6.5 0.7 all-gather.7.cloned.1.call-update
  7.3 0.7 all-gather.5.cloned.1.call-update
  8.1 0.7 all-gather.11.cloned.1.call-update
  8.9 1.0 multiply_cosine_fusion
  9.9 1.9 fusion.15
  11.8 1.9 fusion.17
  13.7 71.1 %all-gather.7.cloned.1.call-done = bf16[5376,2,512]{2,1,0:T(2,128)(2,1)} async-done(((bf16[1344,2,512]{2,1,0:T(2,128)(2,1)}), bf16[5376,2,512]{2,1,0:T(2,128)(2,1)}) %all-gather.7.cloned.1.call-update) | async-done | bytes 11010064 | tf_op jit(solution)/shard_map/all_gather | solution.py:64
  84.8 27.7 %copy.39 = bf16[5376,2,512]{0,2,1:T(8,128)(2,1)} copy(bf16[5376,2,512]{2,1,0:T(2,128)(2,1)} %all-gather.7.cloned.1.call-done) | data formatting | bytes 22020096 | tf_op jit(solution)/shard_map/reshape | solution.py:64
  112.5 166.4 %all-gather.5.cloned.1.call-done = bf16[1024,5376]{0,1:T(8,128)(2,1)} async-done(((bf16[1024,1344]{0,1:T(8,128)(2,1)}), bf16[1024,5376]{0,1:T(8,128)(2,1)}) %all-gather.5.cloned.1.call-update) | async-done | bytes 11010064 | tf_op jit(solution)/shard_map/all_gather | solution.py:67
  278.9 15.9 %fusion.2 = f32[1024,2,4,128]{0,3,2,1:T(8,128)S(1)} fusion(bf16[2,4,128,5376]{3,2,1,0:T(8,128)(2,1)} %bitcast.101, bf16[1024,5376]{0,1:T(8,128)(2,1)} %all-gather.5.cloned.1.call-done), kind=kOutput, calls=%fused_computation.8 | convolution fusion | flops 11274289152 | bytes 26214400 | tf_op jit(solution)/shard_map/dot_general | solution.py:66
  295.1 0.2 multiply_multiply_fusion.1
  295.5 2.2 collective-permute-start
  297.8 0.2 multiply_reduce_fusion
  298.0 0.4 multiply_multiply_fusion
  298.5 1.4 subtract_convert_fusion
  300.0 0.2 fusion.18
  300.2 10.3 %fusion.45 = (f32[2,2,512]{2,1,0:T(2,128)S(1)}, f32[2,2,512,1536]{2,3,1,0:T(8,128)}) fusion(pred[512,1536]{0,1:T(8,128)(4,1)} %fusion.17, bf16[1536,2,2,128]{0,3,2,1:T(8,128)(2,1)S(1)} %bitcast.105, bf16[1024,2,2,64]{0,3,2,1:T(8,128)(2,1)} %get-tuple-element.6, bf16[1024,2,2,64]{0,3,2,1:T(8,128)(2,1)} %get-tuple-element.5), kind=kOutput, calls=%fused_computation.80 | convolution fusion | flops 822085120 | bytes 15998976 | tf_op jit(solution)/shard_map/sub | solution.py:53
  310.6 10.2 %fusion.46 = (f32[2,2,512]{2,1,0:T(2,128)S(1)}, f32[2,2,512,1536]{2,3,1,0:T(8,128)}) fusion(pred[512,1536]{0,1:T(8,128)(4,1)} %fusion.15, bf16[1536,2,2,128]{0,3,2,1:T(8,128)(2,1)S(1)} %bitcast.107, bf16[1024,2,2,64]{0,3,2,1:T(8,128)(2,1)} %get-tuple-element.5, bf16[1024,2,2,64]{0,3,2,1:T(8,128)(2,1)} %get-tuple-element.6), kind=kOutput, calls=%fused_computation.81 | convolution fusion | flops 822085120 | bytes 15998976 | tf_op jit(solution)/shard_map/sub | solution.py:53
  320.8 5.7 %fusion.25 = bf16[512,2,2,128]{0,3,2,1:T(8,128)(2,1)S(1)} fusion(f32[2,2,512,1536]{2,3,1,0:T(8,128)} %get-tuple-element.16, f32[2,2,512]{2,1,0:T(2,128)S(1)} %get-tuple-element.15, bf16[1536,2,2,128]{0,3,2,1:T(8,128)(2,1)S(1)} %bitcast.108), kind=kOutput, calls=%fused_computation.37 | convolution fusion | flops 811859968 | bytes 13901824 | tf_op jit(solution)/shard_map/hgqk,khd->qhgd/dot_general | solution.py:56
  326.5 2.4 copy-done.2
  329.0 1.0 fusion.26
  330.0 1.1 pad_maximum_fusion.2
  331.1 111.1 %all-gather.9.cloned.1.call-done = bf16[1024,2048]{0,1:T(8,128)(2,1)} async-done(((bf16[1024,512]{0,1:T(8,128)(2,1)}), bf16[1024,2048]{0,1:T(8,128)(2,1)}) %all-gather.9.cloned.1.call-update) | async-done | bytes 4194320 | tf_op jit(solution)/shard_map/all_gather | solution.py:105
  442.3 10.1 %convolution_convert_fusion = bf16[1024,1344]{0,1:T(8,128)(2,1)} fusion(bf16[2048,1344]{0,1:T(8,128)(2,1)} %all-gather.11.cloned.1.call-done, bf16[1024,2048]{0,1:T(8,128)(2,1)} %all-gather.9.cloned.1.call-done), kind=kOutput, calls=%fused_computation.20 | convolution fusion | flops 5638520832 | bytes 12451840 | tf_op jit(solution)/shard_map/dot_general | solution.py:104
  (26 shorter events, 0.8 us)
Async XLA Ops:
  6.5 78.3 %all-gather.7.cloned.1.call-start = ((), (), s32[]{:S(2)}) async-start(), calls=%async_computation.1 | async-start | bytes 13762560 | tf_op jit(solution)/shard_map/all_gather | solution.py:64
  7.3 271.7 %all-gather.5.cloned.1.call-start = ((), (), s32[]{:S(2)}) async-start(), calls=%async_computation | async-start | bytes 13762560 | tf_op jit(solution)/shard_map/all_gather | solution.py:67
  8.0 323.1 %all-gather.11.cloned.1.call-start = ((), (), s32[]{:S(2)}) async-start(), calls=%async_computation.3 | async-start | bytes 6881280 | tf_op jit(solution)/shard_map/all_gather | solution.py:102
  8.7 433.5 %all-gather.9.cloned.1.call-start = ((), (), s32[]{:S(2)}) async-start(), calls=%async_computation.2 | async-start | bytes 5242880 | tf_op jit(solution)/shard_map/all_gather | solution.py:105
  278.9 16.2 %copy-start = (f32[128]{0:T(128)S(1)}, f32[128]{0:T(128)}, u32[]{:S(2)}) copy-start(f32[128]{0:T(128)} %param.9) | copy-start | bytes 1540
  295.1 3.0 copy-start.1
  295.5 4.4 collective-permute-start
  320.8 8.2 %copy-start.2 = (f32[2,2,512,1536]{2,3,1,0:T(8,128)S(1)}, f32[2,2,512,1536]{2,3,1,0:T(8,128)}, u32[]{:S(2)}) copy-start(f32[2,2,512,1536]{2,3,1,0:T(8,128)} %get-tuple-element.14) | copy-start | bytes 37748740
Sparse Core Ops, SparseCore 0:
  8.9 75.8 all-gather.6
  86.4 192.4 all-gather.4
  280.5 45.1 all-gather.10
  331.2 110.9 all-gather.8
where the time goes:
time: 460 us; the launch traced here: 459 us
  waiting for transfers between devices  351 us (76%)
  matrix products  53.4 us (12%)
  local copies, waits for them, and re-layouts  30.2 us (7%)
  between operations  13.3 us (3%)
  other arithmetic  8.83 us (2%)
    all_gather x1, waiting for transfers between devices, on_device(): lax.all_gather(states, 'hid', axis=1, tiled=True)  166 us
    all_gather x1, waiting for transfers between devices, on_device(): lax.all_gather(heads_out, 'hid', axis=1, tiled=True)  111 us
    all_gather x1, waiting for transfers between devices, on_device(): lax.all_gather(w_qkv, 'tok', axis=0, tiled=True).reshape(-1, columns)  71.1 us
    reshape x1, local copies, waits for them, and re-layouts, on_device(): lax.all_gather(w_qkv, 'tok', axis=0, tiled=True).reshape(-1, columns)  27.7 us
    sub x2, matrix products, attend(): expo = jnp.where(keep, jnp.exp(masked - top), jnp.float32(0.0))  20.6 us
    dot_general x1, matrix products, on_device(): jnp.dot(lax.all_gather(states, 'hid', axis=1, tiled=True), weight_part, p...  15.9 us
    dot_general x1, matrix products, on_device(): jnp.dot(lax.all_gather(heads_out, 'hid', axis=1, tiled=True), weight_part...  10.1 us
  transfers between devices with their start and end apart: 5, of which 4 were waited for; matrix products, arithmetic and copies ran while one was open for 17% of the time, Pallas kernels for 0%

commit v1 on v0

--- a/solution.py
+++ b/solution.py
@@ -10,6 +10,19 @@
 EPS = 1e-06
 SCALE = 168.0 ** (-0.5)
 ROPE_BASE = 10000.0
+
+
+def gather_around(array, axis, dim):
+    ways = lax.axis_size(axis)
+    up = [(d, (d + 1) % ways) for d in range(ways)]
+    down = [(d, (d - 1) % ways) for d in range(ways)]
+    earlier, later = ([array], [array])
+    for _ in range(ways // 2):
+        earlier.append(lax.ppermute(earlier[-1], axis, up))
+    for _ in range((ways - 1) // 2):
+        later.append(lax.ppermute(later[-1], axis, down))
+    line = jnp.concatenate([*earlier[::-1], *later[1:]], axis=dim)
+    return jnp.roll(line, (lax.axis_index(axis) - ways // 2) * array.shape[dim], axis=dim)
 
 
 def from_behind(value, axis, steps):
@@ -63,11 +76,7 @@
     columns = kv_local * (GROUP + 2) * HD
     weight_whole = lax.all_gather(w_qkv, "tok", axis=0, tiled=True).reshape(-1, columns)
     weight_part = weight_whole
-    qkv = jnp.dot(
-        lax.all_gather(states, "hid", axis=1, tiled=True),
-        weight_part,
-        preferred_element_type=jnp.float32,
-    )
+    qkv = jnp.dot(gather_around(states, "hid", 1), weight_part, preferred_element_type=jnp.float32)
     qkv = qkv.reshape(rows, kv_local, GROUP + 2, HD)
     base = lax.axis_index("tok") * rows
     pos = base + jnp.arange(rows, dtype=jnp.int32)

time: 460 us -> 430 us (0.935)
  waiting for transfers between devices: 351 us -> 254 us
  local copies, waits for them, and re-layouts: 30.2 us -> 88.5 us
    all_gather x1 -> x0, waiting for transfers between devices: 166 us -> none  [on_device(): lax.all_gather(states, 'hid', axis=1, tiled=True)]
    ppermute x0 -> x3, waiting for transfers between devices: none -> 161 us  [the longest x2 116 us: gather_around(): earlier.append(lax.ppermute(earlier[-1], axis, up))]
    all_gather x1, waiting for transfers between devices: 71.1 us -> 0.01 us  [on_device(): lax.all_gather(w_qkv, 'tok', axis=0, tiled=True).reshape(-1, columns)]
    concatenate x0 -> x1, local copies, waits for them, and re-layouts: none -> 41.7 us  [gather_around(): jnp.roll(line, (lax.axis_index(axis) - ways // 2) * array.shape[dim], axi...]
    all_gather x1, waiting for transfers between devices: 111 us -> 92.6 us  [on_device(): lax.all_gather(heads_out, 'hid', axis=1, tiled=True)]
    ppermute x0 -> x3, local copies, waits for them, and re-layouts: none -> 13.6 us  [the longest x2 9.06 us: gather_around(): earlier.append(lax.ppermute(earlier[-1], axis, up))]
    ppermute x0 -> x3, starting transfers between devices: none -> 5.17 us  [the longest x2 3.08 us: gather_around(): earlier.append(lax.ppermute(earlier[-1], axis, up))]
  transfers between devices with their start and end apart: 5 -> 7, of which waited for: 4 -> 4; matrix products, arithmetic and copies ran while one was open for 17% -> 33% of each run, Pallas kernels for 0% -> 0%
where the time goes in v1:
time: 430 us; the launch traced here: 425 us
  waiting for transfers between devices  254 us (59%)
  local copies, waits for them, and re-layouts  88.5 us (21%)
  matrix products  53.3 us (12%)
  between operations  13.4 us (3%)
  other arithmetic  8.84 us (2%)
  starting transfers between devices  6.79 us (2%)
    ppermute x2, waiting for transfers between devices, gather_around(): earlier.append(lax.ppermute(earlier[-1], axis, up))  116 us
    all_gather x1, waiting for transfers between devices, on_device(): lax.all_gather(heads_out, 'hid', axis=1, tiled=True)  92.6 us
    ppermute x1, waiting for transfers between devices, gather_around(): later.append(lax.ppermute(later[-1], axis, down))  44.9 us
    concatenate x1, local copies, waits for them, and re-layouts, gather_around(): jnp.roll(line, (lax.axis_index(axis) - ways // 2) * array.shape[dim], axi...  41.7 us
    reshape x1, local copies, waits for them, and re-layouts, on_device(): lax.all_gather(w_qkv, 'tok', axis=0, tiled=True).reshape(-1, columns)  27.4 us
    sub x2, matrix products, attend(): expo = jnp.where(keep, jnp.exp(masked - top), jnp.float32(0.0))  20.6 us
    dot_general x1, matrix products, on_device(): jnp.dot(gather_around(states, 'hid', 1), weight_part, preferred_element_t...  15.9 us
    dot_general x1, matrix products, on_device(): jnp.dot(lax.all_gather(heads_out, 'hid', axis=1, tiled=True), weight_part...  10.1 us
  transfers between devices with their start and end apart: 7, of which 4 were waited for; matrix products, arithmetic and copies ran while one was open for 33% of the time, Pallas kernels for 0%

profile of v1, /device:TPU:0, one launch (start us, length us, event | category | flops | bytes accessed | tf_op | source)
XLA Modules:
  0.0 424.8 jit_solution(5283161865980007829)
XLA Ops:
  7.3 3.1 collective-permute-start
  10.4 2.1 collective-permute-start.2
  12.5 60.8 %collective-permute-done = bf16[1024,1344]{0,1:T(8,128)(2,1)} collective-permute-done((bf16[1024,1344]{0,1:T(8,128)(2,1)}, bf16[1024,1344]{0,1:T(8,128)(2,1)}, u32[]{:S(2)}, u32[]{:S(2)}) %collective-permute-start) | collective-permute-done | bytes 2752544 | tf_op jit(solution)/shard_map/ppermute | solution.py:21
  73.4 3.3 copy.32
  77.8 1.9 fusion.16
  79.7 1.9 fusion.18
  81.6 4.5 %copy.31 = bf16[1024,1344]{1,0:T(8,128)(2,1)} copy(bf16[1024,1344]{0,1:T(8,128)(2,1)} %collective-permute-done) | data formatting | bytes 5505024 | tf_op jit(solution)/shard_map/ppermute | solution.py:21
  86.1 44.9 %collective-permute-done.2 = bf16[1024,1344]{0,1:T(8,128)(2,1)} collective-permute-done((bf16[1024,1344]{0,1:T(8,128)(2,1)}, bf16[1024,1344]{0,1:T(8,128)(2,1)}, u32[]{:S(2)}, u32[]{:S(2)}) %collective-permute-start.2) | collective-permute-done | bytes 2752544 | tf_op jit(solution)/shard_map/ppermute | solution.py:23
  131.0 4.5 %copy.33 = bf16[1024,1344]{1,0:T(8,128)(2,1)} copy(bf16[1024,1344]{0,1:T(8,128)(2,1)} %collective-permute-done.2) | data formatting | bytes 5505024 | tf_op jit(solution)/shard_map/ppermute | solution.py:23
  135.5 54.9 %collective-permute-done.1 = bf16[1024,1344]{0,1:T(8,128)(2,1)} collective-permute-done((bf16[1024,1344]{0,1:T(8,128)(2,1)}, bf16[1024,1344]{0,1:T(8,128)(2,1)}, u32[]{:S(2)}, u32[]{:S(2)}) %collective-permute-start.1) | collective-permute-done | bytes 2752544 | tf_op jit(solution)/shard_map/ppermute | solution.py:21
  190.4 4.5 %copy.30 = bf16[1024,1344]{1,0:T(8,128)(2,1)} copy(bf16[1024,1344]{0,1:T(8,128)(2,1)} %collective-permute-done.1) | data formatting | bytes 5505024 | tf_op jit(solution)/shard_map/ppermute | solution.py:21
  194.9 41.7 %concatenate.31 = bf16[1024,10752]{1,0:T(8,128)(2,1)} concatenate(bf16[1024,1344]{1,0:T(8,128)(2,1)} %copy.30, bf16[1024,1344]{1,0:T(8,128)(2,1)} %copy.31, bf16[1024,1344]{1,0:T(8,128)(2,1)S(1)} %copy.32, bf16[1024,1344]{1,0:T(8,128)(2,1)} %copy.33, bf16[1024,1344]{1,0:T(8,128)(2,1)} %copy.30, bf16[1024,1344]{1,0:T(8,128)(2,1)} %copy.31, bf16[1024,1344]{1,0:T(8,128)(2,1)S(1)} %copy.32, ...), dimensions={1} | concatenate | bytes 44040192 | tf_op jit(solution)/shard_map/jit(_roll_dynamic)/concatenate | solution.py:25
  236.7 27.4 %copy.55 = bf16[5376,2,512]{0,2,1:T(8,128)(2,1)} copy(bf16[5376,2,512]{2,1,0:T(2,128)(2,1)} %all-gather.4.cloned.1.call-done) | data formatting | bytes 22020096 | tf_op jit(solution)/shard_map/reshape | solution.py:77
  264.1 15.9 %fusion.2 = f32[1024,2,4,128]{0,3,2,1:T(8,128)S(1)} fusion(bf16[2,4,128,5376]{3,2,1,0:T(8,128)(2,1)} %bitcast.101, bf16[1024,10752]{1,0:T(8,128)(2,1)} %concatenate.31, s32[]{:T(128)S(6)} %select_n.27), kind=kOutput, calls=%fused_computation.8 | convolution fusion | flops 11274289152 | bytes 26214404 | tf_op jit(solution)/shard_map/dot_general | solution.py:79
  280.6 1.5 collective-permute-start.3
  282.9 1.4 subtract_convert_fusion
  284.5 10.3 %fusion.47 = (f32[2,2,512]{2,1,0:T(2,128)S(1)}, f32[2,2,512,1536]{2,3,1,0:T(8,128)}) fusion(pred[512,1536]{0,1:T(8,128)(4,1)} %fusion.18, bf16[1536,2,2,128]{0,3,2,1:T(8,128)(2,1)S(1)} %bitcast.105, bf16[1024,2,2,64]{0,3,2,1:T(8,128)(2,1)} %get-tuple-element.6, bf16[1024,2,2,64]{0,3,2,1:T(8,128)(2,1)} %get-tuple-element.5), kind=kOutput, calls=%fused_computation.82 | convolution fusion | flops 822085120 | bytes 15998976 | tf_op jit(solution)/shard_map/sub | solution.py:66
  294.9 10.2 %fusion.48 = (f32[2,2,512]{2,1,0:T(2,128)S(1)}, f32[2,2,512,1536]{2,3,1,0:T(8,128)}) fusion(pred[512,1536]{0,1:T(8,128)(4,1)} %fusion.16, bf16[1536,2,2,128]{0,3,2,1:T(8,128)(2,1)S(1)} %bitcast.107, bf16[1024,2,2,64]{0,3,2,1:T(8,128)(2,1)} %get-tuple-element.5, bf16[1024,2,2,64]{0,3,2,1:T(8,128)(2,1)} %get-tuple-element.6), kind=kOutput, calls=%fused_computation.83 | convolution fusion | flops 822085120 | bytes 15998976 | tf_op jit(solution)/shard_map/sub | solution.py:66
  305.1 5.7 %fusion.26 = bf16[512,2,2,128]{0,3,2,1:T(8,128)(2,1)S(1)} fusion(f32[2,2,512,1536]{2,3,1,0:T(8,128)} %get-tuple-element.16, f32[2,2,512]{2,1,0:T(2,128)S(1)} %get-tuple-element.15, bf16[1536,2,2,128]{0,3,2,1:T(8,128)(2,1)S(1)} %bitcast.108), kind=kOutput, calls=%fused_computation.38 | convolution fusion | flops 811859968 | bytes 13901824 | tf_op jit(solution)/shard_map/hgqk,khd->qhgd/dot_general | solution.py:69
  310.9 2.4 copy-done.2
  313.3 1.0 fusion.27
  314.3 1.1 pad_maximum_fusion.2
  315.5 92.6 %all-gather.6.cloned.1.call-done = bf16[1024,2048]{0,1:T(8,128)(2,1)} async-done(((bf16[1024,512]{0,1:T(8,128)(2,1)}), bf16[1024,2048]{0,1:T(8,128)(2,1)}) %all-gather.6.cloned.1.call-update) | async-done | bytes 4194320 | tf_op jit(solution)/shard_map/all_gather | solution.py:114
  408.1 10.1 %convolution_convert_fusion = bf16[1024,1344]{0,1:T(8,128)(2,1)} fusion(bf16[2048,1344]{0,1:T(8,128)(2,1)} %all-gather.8.cloned.1.call-done, bf16[1024,2048]{0,1:T(8,128)(2,1)} %all-gather.6.cloned.1.call-done), kind=kOutput, calls=%fused_computation.21 | convolution fusion | flops 5638520832 | bytes 12451840 | tf_op jit(solution)/shard_map/dot_general | solution.py:113
  (34 shorter events, 3.5 us)
Async XLA Ops:
  6.5 230.1 %all-gather.4.cloned.1.call-start = ((), (), s32[]{:S(2)}) async-start(), calls=%async_computation | async-start | bytes 13762560 | tf_op jit(solution)/shard_map/all_gather | solution.py:77
  7.3 308.2 %all-gather.8.cloned.1.call-start = ((), (), s32[]{:S(2)}) async-start(), calls=%async_computation.2 | async-start | bytes 6881280 | tf_op jit(solution)/shard_map/all_gather | solution.py:111
  7.3 66.0 %collective-permute-start = (bf16[1024,1344]{0,1:T(8,128)(2,1)}, bf16[1024,1344]{0,1:T(8,128)(2,1)}, u32[]{:S(2)}, u32[]{:S(2)}) collective-permute-start(bf16[1024,1344]{0,1:T(8,128)(2,1)} %param.5), channel_id=1, source_target_pairs={{0,1},{1,2},{2,3},{3,0},{4,5},{5,6},{6,7},{7,4},{8,9},{9,10},{10,1... | collective-permute-start | bytes 8257544 | tf_op jit(solution)/shard_map/ppermute | solution.py:21
  10.4 120.6 %collective-permute-start.2 = (bf16[1024,1344]{0,1:T(8,128)(2,1)}, bf16[1024,1344]{0,1:T(8,128)(2,1)}, u32[]{:S(2)}, u32[]{:S(2)}) collective-permute-start(bf16[1024,1344]{0,1:T(8,128)(2,1)} %param.5), channel_id=1, source_target_pairs={{0,3},{1,0},{2,1},{3,2},{4,7},{5,4},{6,5},{7,6},{8,11},{9,8},{10,9... | collective-permute-start | bytes 8257544 | tf_op jit(solution)/shard_map/ppermute | solution.py:23
  73.3 117.1 %collective-permute-start.1 = (bf16[1024,1344]{0,1:T(8,128)(2,1)}, bf16[1024,1344]{0,1:T(8,128)(2,1)}, u32[]{:S(2)}, u32[]{:S(2)}) collective-permute-start(bf16[1024,1344]{0,1:T(8,128)(2,1)} %collective-permute-done), channel_id=1, source_target_pairs={{0,1},{1,2},{2,3},{3,0},{4,5},{5,6},{6,7},{7,4},{8,9},{9,10},{10,1... | collective-permute-start | bytes 8257544 | tf_op jit(solution)/shard_map/ppermute | solution.py:21
  73.3 334.8 %all-gather.6.cloned.1.call-start = ((), (), s32[]{:S(2)}) async-start(), calls=%async_computation.1 | async-start | bytes 5242880 | tf_op jit(solution)/shard_map/all_gather | solution.py:114
  264.1 16.1 %copy-start = (f32[128]{0:T(128)S(1)}, f32[128]{0:T(128)}, u32[]{:S(2)}) copy-start(f32[128]{0:T(128)} %param.9) | copy-start | bytes 1540
  280.4 2.1 copy-start.1
  280.6 3.7 collective-permute-start.3
  305.1 8.2 %copy-start.2 = (f32[2,2,512,1536]{2,3,1,0:T(8,128)S(1)}, f32[2,2,512,1536]{2,3,1,0:T(8,128)}, u32[]{:S(2)}) copy-start(f32[2,2,512,1536]{2,3,1,0:T(8,128)} %get-tuple-element.14) | copy-start | bytes 37748740
Sparse Core Ops, SparseCore 0:
  8.9 75.8 all-gather.3
  86.4 86.0 all-gather.7
  315.5 92.4 all-gather.5
